TPU v7x, 128 devices: a whole 4x4x4 slice. The times are simulated.
128 devices in a mesh: tok: 16 (over x, y), exp: 8 (over z, core).
Axes of the slice: x: 4, y: 4, z: 4, core: 2. Of those that a mesh axis runs over, the one named last changes fastest.
Arguments:
- tokens: bfloat16 [57344, 1536], P('tok'), may hold values from -9 to 9
- dispatch_keys: bfloat16 [512, 1536], P(('tok', 'exp')), may hold values from -0.33458226 to 0.33458226
- expand_weight: bfloat16 [512, 1536, 512], P(('tok', 'exp')), may hold values from -0.15625 to 0.15625
- reduce_weight: bfloat16 [512, 512, 1536], P(('tok', 'exp')), may hold values from -0.25 to 0.25
- teacher: bfloat16 [57344, 1536], P(('tok', 'exp')), may hold values from -9 to 9
Outputs:
- mixed: bfloat16 [57344, 1536], P(('tok', 'exp'))
- loss: float32 [], replicated
- grad_keys: float32 [512, 1536], P(('tok', 'exp'))
All inputs are finite; a program needn't handle non-finite values.
Results may differ from a plain program's by a relative error of at most 0.04.
Values may be sent and summed in bfloat16 or wider, within the bound.
A program may use at most 128 MiB of HBM per device.

v0:
```python
import jax
import jax.numpy as jnp
from jax import lax
from jax.sharding import PartitionSpec as P

gelu_coef = 0.7978845608028654
cube_coef = 0.044715


def gelu_pair(values):
    tanh_value = jnp.tanh(gelu_coef * (values + cube_coef * values * values * values))
    output = 0.5 * values * (1.0 + tanh_value)
    derivative = 0.5 * (1.0 + tanh_value) + 0.5 * values * (
        1.0 - tanh_value * tanh_value
    ) * gelu_coef * (1.0 + 3.0 * cube_coef * values * values)
    return (output, derivative)


def contract_last(left, right):
    return lax.dot_general(
        left, right, (((1,), (1,)), ((), ())), preferred_element_type=jnp.float32
    )


def contract_first(left, right):
    return lax.dot_general(
        left, right, (((0,), (0,)), ((), ())), preferred_element_type=jnp.float32
    )


def body(tokens, dispatch_keys, expand_weight, reduce_weight, teacher):
    tok_count = lax.axis_size("tok")
    tok_rows = tokens.shape[0]
    part_rows = teacher.shape[0]
    model_width = tokens.shape[1]
    all_keys = lax.all_gather(dispatch_keys, ("tok", "exp"), axis=0, tiled=True)
    group_keys = lax.all_gather(dispatch_keys, "tok", axis=0, tiled=True)
    logits = contract_last(group_keys, tokens)
    col_max = lax.pmax(jnp.max(logits, axis=1), "tok")
    exp_terms = jnp.exp(logits - col_max[:, None])
    weighted = jnp.dot(exp_terms.astype(jnp.bfloat16), tokens, preferred_element_type=jnp.float32)
    slot_sum, slot_total = (
        lax.psum_scatter(weighted, "tok", scatter_dimension=0, tiled=True),
        lax.psum_scatter(jnp.sum(exp_terms, axis=1), "tok", scatter_dimension=0, tiled=True),
    )
    slot_in = slot_sum / slot_total[:, None]
    root_mean = jnp.sqrt(jnp.mean(slot_in * slot_in, axis=1, keepdims=True) + 1e-06)
    normed = slot_in / root_mean
    pre_act = jnp.einsum(
        "ed,edh->eh", normed.astype(jnp.bfloat16), expand_weight, preferred_element_type=jnp.float32
    )
    act_value, gelu_slope = gelu_pair(pre_act)
    slot_out = jnp.einsum(
        "eh,ehd->ed",
        act_value.astype(jnp.bfloat16),
        reduce_weight,
        preferred_element_type=jnp.float32,
    ).astype(jnp.bfloat16)
    every_out = lax.all_gather(slot_out, ("tok", "exp"), axis=0, tiled=True)
    local_rows = lax.dynamic_slice_in_dim(tokens, lax.axis_index("exp") * part_rows, part_rows, 0)
    scores = contract_last(local_rows, all_keys)
    row_terms = jnp.exp(scores - jnp.max(scores, axis=1, keepdims=True))
    comb = row_terms / jnp.sum(row_terms, axis=1, keepdims=True)
    comb_b = comb.astype(jnp.bfloat16)
    result = jnp.dot(comb_b, every_out, preferred_element_type=jnp.float32)
    mixed = result.astype(jnp.bfloat16)
    misfit = result - teacher.astype(jnp.float32)
    loss_total = lax.psum(jnp.sum(misfit * misfit), ("tok", "exp"))
    loss = loss_total / (2.0 * tok_rows * tok_count * model_width)
    grad_rows = (misfit / model_width).astype(jnp.bfloat16)
    dcomb = contract_last(grad_rows, every_out)
    dscore = (comb * (dcomb - jnp.sum(comb * dcomb, axis=1, keepdims=True))).astype(jnp.bfloat16)
    out_part = contract_first(comb_b, grad_rows)
    key_part = contract_first(dscore, local_rows)
    key_comb, out_grad = (
        lax.psum_scatter(key_part, ("tok", "exp"), scatter_dimension=0, tiled=True),
        lax.psum_scatter(out_part, ("tok", "exp"), scatter_dimension=0, tiled=True),
    )
    dact = jnp.einsum(
        "ed,ehd->eh",
        out_grad.astype(jnp.bfloat16),
        reduce_weight,
        preferred_element_type=jnp.float32,
    )
    dpre = (dact * gelu_slope).astype(jnp.bfloat16)
    dnormed = jnp.einsum("eh,edh->ed", dpre, expand_weight, preferred_element_type=jnp.float32)
    dslot = (dnormed - normed * jnp.mean(dnormed * normed, axis=1, keepdims=True)) / root_mean
    scaled_b = (dslot / slot_total[:, None]).astype(jnp.bfloat16)
    group_scaled = lax.all_gather(scaled_b, "tok", axis=0, tiled=True)
    full_terms = jnp.exp(logits - col_max[:, None])
    dprob = contract_last(group_scaled, tokens)
    dlogit = (full_terms * dprob).astype(jnp.bfloat16)
    term = jnp.dot(dlogit, tokens, preferred_element_type=jnp.float32)
    key_disp = lax.psum_scatter(term, "tok", scatter_dimension=0, tiled=True)
    grad_sum = key_comb + key_disp
    grad_keys = grad_sum / model_width**0.5
    return (mixed, loss, grad_keys)


def solution(mesh):
    in_specs = (
        P("tok", None),
        P(("tok", "exp"), None),
        P(("tok", "exp"), None, None),
        P(("tok", "exp"), None, None),
        P(("tok", "exp"), None),
    )
    out_specs = (P(("tok", "exp"), None), P(), P(("tok", "exp"), None))
    return jax.shard_map(body, mesh=mesh, in_specs=in_specs, out_specs=out_specs, check_vma=False)
```

profile of v0, /device:TPU:1, one launch (start us, length us, event | category | flops | bytes accessed | tf_op | source)
XLA Modules:
  0.0 650.7 jit_solution(9596174491972240049)
XLA Ops:
  8.0 0.0 all-reduce.11.cloned.1.call-start
  8.0 19.7 %all-gather.1 = bf16[16,4,1536]{2,1,0:T(4,128)(2,1)S(1)} all-gather(bf16[1,4,1536]{2,1,0:T(4,128)(2,1)} %bitcast.64), channel_id=1, replica_groups=mesh['tok'=16,'exp'=8] {'tok'}, dimensions={0}, use_global_device_ids=true | all-gather | bytes 208896 | tf_op jit(solution)/shard_map/all_gather | solution.py:37
  27.7 0.1 reshape.26
  27.8 7.6 %fusion.50 = (f32[64]{0:T(128)S(1)}, f32[64,3584]{1,0:T(8,128)S(1)}) fusion(bf16[64,1536]{1,0:T(8,128)(2,1)S(1)} %reshape.26, bf16[3584,1536]{1,0:T(8,128)(2,1)} %param.5), kind=kOutput, calls=%fused_computation.68 | convolution fusion | flops 704872384 | bytes 12124416 | tf_op jit(solution)/shard_map/dot_general | solution.py:20
  35.4 30.9 %pmax.7 = f32[64]{0:T(128)S(1)} all-reduce(f32[64]{0:T(128)S(1)} %get-tuple-element.9), channel_id=1, replica_groups=mesh['tok'=16,'exp'=8] {'tok'}, use_global_device_ids=true, to_apply=%region_3.0 | all-reduce | flops 64 | bytes 512 | tf_op jit(solution)/shard_map/pmax | solution.py:39
  66.3 0.0 copy-start.1
  66.3 7.0 %fusion.10 = f32[64,1536]{1,0:T(8,128)} fusion(bf16[3584,1536]{1,0:T(8,128)(2,1)} %param.5, f32[64,3584]{1,0:T(8,128)S(1)} %get-tuple-element.10, f32[64]{0:T(128)S(1)} %pmax.7), kind=kOutput, calls=%fused_computation.18 | convolution fusion | flops 705101824 | bytes 12321024 | tf_op jit(solution)/shard_map/dot_general | solution.py:41
  73.3 0.0 all-reduce.11.cloned.1.call-update
  73.3 0.0 all-gather.7.cloned.1.call-start
  73.4 0.5 all-gather.7.cloned.1.call-update
  73.9 0.0 all-gather.9.cloned.1.call-start
  74.0 0.0 copy-done.1
  74.0 0.6 dynamic-slice
  75.2 0.3 fusion.7
  75.5 28.7 %all-reduce.1 = f32[64]{0:T(128)S(1)} all-reduce(f32[64]{0:T(128)S(1)} %fusion.7), channel_id=3, replica_groups=mesh['tok'=16,'exp'=8] {'tok'}, use_global_device_ids=true, to_apply=%region_6.0.clone | all-reduce | flops 64 | bytes 512
  104.2 0.1 dynamic-slice.3
  104.3 61.7 %all-reduce.11.cloned.1.call-done = f32[64,1536]{1,0:T(8,128)} async-done(((f32[64,1536]{1,0:T(8,128)}), f32[64,1536]{1,0:T(8,128)}) %all-reduce.11.cloned.1.call-update) | async-done | bytes 393232
  166.0 1.0 fusion.26
  167.0 0.1 sqrt_multiply_fusion
  167.1 0.9 convert_bitcast_fusion
  167.9 3.7 fusion.24
  171.7 3.7 fusion.40
  175.4 0.6 copy.45
  176.0 0.0 all-gather.9.cloned.1.call-update
  176.0 0.0 all-reduce.15.cloned.1.call-start
  176.1 0.0 all-gather.7.cloned.1.call-done
  176.1 2.7 reshape.24
  178.9 2.3 fusion.51
  181.2 0.3 fusion.6
  181.5 60.1 %all-gather.9.cloned.1.call-done = bf16[128,4,1536]{2,1,0:T(4,128)(2,1)} async-done(((bf16[1,4,1536]{2,1,0:T(4,128)(2,1)}), bf16[128,4,1536]{2,1,0:T(4,128)(2,1)}) %all-gather.9.cloned.1.call-update) | async-done | bytes 1572880 | tf_op jit(solution)/shard_map/all_gather | solution.py:59
  241.6 2.7 reshape.28
  244.3 0.0 copy-start
  244.4 4.1 multiply_reduce_fusion
  248.5 0.0 copy-start.2
  248.5 0.0 copy-done
  248.5 2.9 fusion.15
  251.3 0.0 copy-done.2
  251.4 99.4 %all-reduce.16 = (f32[]{:T(128)}, bf16[512,1536]{1,0:T(8,128)(2,1)}) all-reduce(f32[]{:T(128)} %get-tuple-element.7, f32[512,1536]{1,0:T(8,128)} %fusion.15), channel_id=1, replica_groups=mesh['tok'=16,'exp'=8] {'tok','exp'}, use_global_device_ids=true, to_apply=%region_9.0 | all-reduce | flops 786433 | bytes 4718600 | tf_op jit(solution)/shard_map/psum | solution.py:68
  350.7 0.7 fusion.29
  351.5 4.5 fusion.22
  356.0 4.5 fusion.38
  360.5 0.1 fusion.20
  360.7 0.1 fusion.30
  360.7 21.1 %all-gather.3 = bf16[16,4,1536]{2,1,0:T(4,128)(2,1)} all-gather(bf16[1,4,1536]{2,1,0:T(4,128)(2,1)S(1)} %fusion.30), channel_id=1, replica_groups=mesh['tok'=16,'exp'=8] {'tok'}, dimensions={0}, use_global_device_ids=true | all-gather | bytes 208896 | tf_op jit(solution)/shard_map/all_gather | solution.py:89
  381.9 1.7 reshape.30
  383.6 13.6 %fusion.9 = f32[64,1536]{1,0:T(8,128)} fusion(bf16[3584,1536]{1,0:T(8,128)(2,1)} %param.5, bf16[64,1536]{1,0:T(8,128)(2,1)} %reshape.30, f32[64,3584]{1,0:T(8,128)S(1)} %get-tuple-element.10, f32[64]{0:T(128)S(1)} %pmax.7), kind=kOutput, calls=%fused_computation.17 | convolution fusion | flops 1409974272 | bytes 12517632 | tf_op jit(solution)/shard_map/dot_general | solution.py:93
  397.2 0.0 all-reduce.15.cloned.1.call-update
  397.2 0.0 all-reduce.13.cloned.1.call-start
  397.3 3.2 multiply_reduce_fusion.1
  400.5 4.3 fusion.1
  404.7 0.0 all-reduce.13.cloned.1.call-update
  405.4 77.0 %all-reduce.15.cloned.1.call-done = f32[64,1536]{1,0:T(8,128)} async-done(((f32[64,1536]{1,0:T(8,128)}), f32[64,1536]{1,0:T(8,128)}) %all-reduce.15.cloned.1.call-update) | async-done | bytes 393232
  482.4 158.7 %all-reduce.13.cloned.1.call-done = f32[512,1536]{1,0:T(8,128)} async-done(((f32[512,1536]{1,0:T(8,128)}), f32[512,1536]{1,0:T(8,128)}) %all-reduce.13.cloned.1.call-update) | async-done | bytes 3145744
  641.0 1.4 fusion.19
  (3 shorter events, 0.1 us)
Async XLA Ops:
  8.0 158.0 %all-reduce.11.cloned.1.call-start = ((), (), s32[]{:S(2)}) async-start(), calls=%async_computation.2 | async-start | bytes 786432
  66.3 7.6 %copy-start.1 = (u32[128]{0:T(128)S(1)}, u32[128]{0:T(128)}, u32[]{:S(2)}) copy-start(u32[128]{0:T(128)} %constant.44) | copy-start | bytes 1540
  73.3 102.8 %all-gather.7.cloned.1.call-start = ((), (), s32[]{:S(2)}) async-start(), calls=%async_computation | async-start | bytes 1585152 | tf_op jit(solution)/shard_map/all_gather | solution.py:36
  73.9 167.7 %all-gather.9.cloned.1.call-start = ((), (), s32[]{:S(2)}) async-start(), calls=%async_computation.1 | async-start | bytes 1585152 | tf_op jit(solution)/shard_map/all_gather | solution.py:59
  176.0 306.3 %all-reduce.15.cloned.1.call-start = ((), (), s32[]{:S(2)}) async-start(), calls=%async_computation.4 | async-start | bytes 786432
  244.3 4.1 copy-start
  248.5 2.9 copy-start.2
  397.2 243.8 %all-reduce.13.cloned.1.call-start = ((), (), s32[]{:S(2)}) async-start(), calls=%async_computation.3 | async-start | bytes 6291456
Sparse Core Ops, SparseCore 0:
  73.4 92.5 all-reduce.10
  397.3 84.9 all-reduce.14
  487.1 153.8 all-reduce.12
Sparse Core Ops, SparseCore 1:
  76.6 74.6 all-gather.6
  176.1 65.4 all-gather.8
where the time goes:
time: 652 us; the launch traced here: 651 us
  waiting for transfers between devices  358 us (55%)
  blocking collectives  200 us (31%)
  matrix products  61.4 us (9%)
  between operations  17.7 us (3%)
  local copies, waits for them, and re-layouts  9.23 us (1%)
    unnamed x8, waiting for transfers between devices  298 us
    psum x1, blocking collectives, body(): loss_total = lax.psum(jnp.sum(misfit * misfit), ('tok', 'exp'))  99.4 us
    all_gather x1, waiting for transfers between devices, body(): every_out = lax.all_gather(slot_out, ('tok', 'exp'), axis=0, tiled=True)  60.1 us
    pmax x1, blocking collectives, body(): col_max = lax.pmax(jnp.max(logits, axis=1), 'tok')  30.9 us
    unnamed x1, blocking collectives  28.7 us
    all_gather x1, blocking collectives, body(): group_scaled = lax.all_gather(scaled_b, 'tok', axis=0, tiled=True)  21.1 us
    all_gather x1, blocking collectives, body(): group_keys = lax.all_gather(dispatch_keys, 'tok', axis=0, tiled=True)  19.7 us
    dot_general x1, matrix products, body(): term = jnp.dot(dlogit, tokens, preferred_element_type=jnp.float32)  13.6 us
  transfers between devices with their start and end apart: 5, of which 4 were waited for; matrix products, arithmetic and copies ran while one was open for 4% of the time, Pallas kernels for 0%

commit v1 on v0

v1 whole, which is shorter than its diff:
```python
import functools
import jax
import jax.numpy as jnp
from jax import lax
from jax.experimental import pallas as pl
from jax.experimental.pallas import tpu as pltpu
from jax.sharding import PartitionSpec as P

MESH = pl.DeviceIdType.MESH
f32, bf16 = jnp.float32, jnp.bfloat16
D, H, ROWS, PART, OWN, GROUP, HALF = 1536, 512, 3584, 448, 4, 64, 256
Q = 384
EXT = 128
CHUNK = 512
gelu_coef = 0.7978845608028654
cube_coef = 0.044715


def gelu_pair(values):
    tanh_value = jnp.tanh(gelu_coef * (values + cube_coef * values * values * values))
    output = 0.5 * values * (1.0 + tanh_value)
    derivative = 0.5 * (1.0 + tanh_value) + 0.5 * values * (
        1.0 - tanh_value * tanh_value
    ) * gelu_coef * (1.0 + 3.0 * cube_coef * values * values)
    return (output, derivative)


def nn(a, b):
    return lax.dot_general(a, b, (((1,), (0,)), ((), ())), preferred_element_type=f32)


def nt(a, b):
    return lax.dot_general(a, b, (((1,), (1,)), ((), ())), preferred_element_type=f32)


def tn(a, b):
    return lax.dot_general(a, b, (((0,), (0,)), ((), ())), preferred_element_type=f32)


def wait_bytes(ref, sem):
    pltpu.make_async_copy(ref, ref, sem).wait()


def kernel(
    tokens_h, keys, expand_h, reduce_h, teacher_h,
    mixed_h, loss_o, grad_o,
    tokens, expand, reduce_, teacher,
    perm, perm_t, stack, wide,
    own_msg, gath_k, all_keys, group_keys,
    terms, weights, partial, msg_b, recv_b,
    normed, x16, out_msg, gath_o, every_out,
    comb, comb_b, grad_rows, mixed,
    half, cross_send, cross_recv, msg_d, recv_d,
    cross_send2, cross_recv2, msg_e, recv_e, loss_own, loss_other,
    f_msg, recv_f, msg_g, recv_g,
    load_sem, mixed_sem, send_k, recv_k, csend_k, crecv_k, send_b, rsem_b,
    send_o, recv_o, csend_o, crecv_o, csend_d, crecv_d, send_d, rsem_d,
    csend_e, crecv_e, send_e, rsem_e, csend_l, crecv_l,
    send_f, rsem_f, send_g, rsem_g,
):
    t = lax.axis_index("tok")
    e = lax.axis_index("exp")
    x, y = lax.div(t, 4), lax.rem(t, 4)
    z, c = lax.div(e, 2), lax.rem(e, 2)
    other = (t, z * 2 + 1 - c)

    loads = [
        pltpu.make_async_copy(tokens_h, tokens, load_sem.at[0]),
        pltpu.make_async_copy(expand_h, expand, load_sem.at[1]),
        pltpu.make_async_copy(reduce_h, reduce_, load_sem.at[2]),
        pltpu.make_async_copy(teacher_h, teacher, load_sem.at[3]),
    ]
    for load in loads:
        load.start()

    def peer(k):
        kt = lax.rem(k, 16)
        x2 = lax.rem(x + lax.div(kt, 4), 4)
        y2 = lax.rem(y + lax.rem(kt, 4), 4)
        z2 = lax.rem(z + lax.div(k, 16), 4)
        return x2 * 4 + y2, z2

    barrier = pltpu.get_barrier_semaphore()

    def greet(k, carry):
        t2, z2 = peer(k)
        pl.semaphore_signal(barrier, inc=1, device_id=(t2, z2 * 2 + c), device_id_type=MESH)
        return carry

    lax.fori_loop(1, 64, greet, 0)
    pl.semaphore_signal(barrier, inc=1, device_id=other, device_id_type=MESH)

    row = lax.broadcasted_iota(jnp.int32, (256, 256), 0)
    col = lax.broadcasted_iota(jnp.int32, (256, 256), 1)

    def moved(r):
        return ((r >> 2) & 15) * 16 + (r >> 6) * 4 + (r & 3)

    perm[...] = jnp.where(col == moved(row), 1.0, 0.0).astype(bf16)
    perm_t[...] = jnp.where(row == moved(col), 1.0, 0.0).astype(bf16)

    def pack(value):
        for j in range(4):
            wide[4 * j : 4 * j + 4, :Q] = value[0:4, Q * j : Q * j + Q]
        return wide[:, :Q]

    def unpack(message):
        wide[:, :Q] = message
        x16[...] = jnp.zeros((16, D), f32)
        for j in range(4):
            x16[0:4, Q * j : Q * j + Q] = wide[4 * j : 4 * j + 4, :Q]

    def spread(rows_, width):
        return nn(perm_t[...], stack[:, :width]).astype(bf16).reshape(16, 16, width)

    def to_stack(value):
        for j in range(4):
            stack[64 * j : 64 * j + 64, :Q] = value[:, Q * j : Q * j + Q].astype(bf16)

    def settle(block, dst, at):
        r = nn(perm[...], block).astype(bf16)
        for j in range(4):
            dst[pl.ds(at, 64), Q * j : Q * j + Q] = r[64 * j : 64 * j + 64]

    def gather_start(src, gath, send, recv):
        pltpu.make_async_copy(src, gath.at[0, z * 16 + t], recv.at[z]).start()

        def step(k, carry):
            t2, z2 = peer(k)
            pltpu.make_async_remote_copy(
                src, gath.at[0, z * 16 + t], send, recv.at[z],
                device_id=(t2, z2 * 2 + c), device_id_type=MESH,
            ).start()
            return carry

        lax.fori_loop(1, 64, step, 0)

    def gather_pass(gath, recv, csend, crecv, dz):
        zz = lax.rem(z + dz, 4)
        part = gath.at[0, pl.ds(zz * 16, 16)]
        wait_bytes(part, recv.at[zz])
        pltpu.make_async_remote_copy(
            part, gath.at[1, pl.ds(zz * 16, 16)], csend.at[zz], crecv.at[zz],
            device_id=other, device_id_type=MESH,
        ).start()
        return zz

    def gather_settle(gath, half_, zz, dst):
        block = gath[half_, pl.ds(zz * 16, 16)].reshape(256, Q)
        settle(block, dst, pl.multiple_of(half_ * 256 + zz * 64, 64))

    def gather_end(gath, send, csend):
        wait_bytes(gath.at[0, pl.ds(0, 63)], send)
        for k in range(4):
            wait_bytes(gath.at[0, pl.ds(0, 16)], csend.at[k])

    def tok_start(src_of, recv_ref, send, recv):
        pltpu.make_async_copy(src_of(t), recv_ref.at[t], recv).start()

        def step(k, carry):
            t2, _ = peer(k)
            pltpu.make_async_remote_copy(
                src_of(t2), recv_ref.at[t], send, recv,
                device_id=(t2, e), device_id_type=MESH,
            ).start()
            return carry

        lax.fori_loop(1, 16, step, 0)

    def all_start(msg, recv_ref, send, recv):
        me = z * 16 + t
        pltpu.make_async_copy(msg.at[me], recv_ref.at[me], recv).start()

        def step(k, carry):
            t2, z2 = peer(k)
            pltpu.make_async_remote_copy(
                msg.at[z2 * 16 + t2], recv_ref.at[me], send, recv,
                device_id=(t2, z2 * 2 + c), device_id_type=MESH,
            ).start()
            return carry

        lax.fori_loop(1, 64, step, 0)

    def gather_sum(ref, n):
        return lax.fori_loop(
            0, n, lambda k, s: s + ref[k].astype(f32), jnp.zeros(ref.shape[1:], f32)
        )

    own_msg[...] = pack(keys[...].astype(f32)).astype(bf16)
    pl.semaphore_wait(barrier, 64)

    gather_start(own_msg, gath_k, send_k, recv_k)
    gather_pass(gath_k, recv_k, csend_k, crecv_k, 0)
    settle(gath_k[0, pl.ds(z * 16, 16)].reshape(256, Q), group_keys, 0)
    loads[0].wait()

    @pl.loop(0, ROWS // CHUNK)
    def _(n):
        at = pl.multiple_of(n * CHUNK, CHUNK)
        terms[:, pl.ds(at, CHUNK)] = nt(group_keys[...], tokens[pl.ds(at, CHUNK), :])

    top = jnp.max(terms[...], axis=1, keepdims=True).astype(bf16).astype(f32)
    exp_terms = jnp.exp(terms[...] - top)
    terms[...] = exp_terms
    weights[...] = exp_terms.astype(bf16)
    total = jnp.sum(exp_terms, axis=1, keepdims=True)

    def column_pass():
        @pl.loop(0, D // 256)
        def _(n):
            at = pl.multiple_of(n * 256, 256)
            partial[:, pl.ds(at, 256)] = nn(weights[...], tokens[:, pl.ds(at, 256)])

    column_pass()
    to_stack(partial[...])
    lane = lax.broadcasted_iota(jnp.int32, (64, EXT), 1)
    total_hi = total.astype(bf16).astype(f32)
    extra = jnp.where(lane == 0, top, jnp.where(lane == 1, total_hi, jnp.where(lane == 2, total - total_hi, 0.0)))
    for j in range(4):
        stack[64 * j : 64 * j + 64, Q:] = extra.astype(bf16)
    msg_b[...] = spread(stack, Q + EXT)
    tok_start(lambda k: msg_b.at[k], recv_b, send_b, rsem_b)

    for dz in range(1, 4):
        gather_pass(gath_k, recv_k, csend_k, crecv_k, dz)
    for k in range(4):
        gather_settle(gath_k, 0, k, all_keys)
    for k in range(4):
        wait_bytes(gath_k.at[1, pl.ds(k * 16, 16)], crecv_k.at[k])
        gather_settle(gath_k, 1, k, all_keys)
    local = tokens.at[pl.ds(pl.multiple_of(e * PART, 64), PART)]
    scores = nt(local[...], all_keys[...])
    row_terms = jnp.exp(scores - jnp.max(scores, axis=1, keepdims=True))
    comb_v = row_terms / jnp.sum(row_terms, axis=1, keepdims=True)
    comb[...] = comb_v
    comb_b[...] = comb_v.astype(bf16)

    wait_bytes(recv_b, rsem_b)
    best = recv_b[0, :, Q : Q + 1].astype(f32)
    for k in range(1, 16):
        best = jnp.maximum(best, recv_b[k, :, Q : Q + 1].astype(f32))
    slot_sum = jnp.zeros((16, Q), f32)
    slot_total = jnp.zeros((16, 1), f32)
    for k in range(16):
        scale = jnp.exp(recv_b[k, :, Q : Q + 1].astype(f32) - best)
        slot_sum += scale * recv_b[k, :, :Q].astype(f32)
        slot_total += scale * (
            recv_b[k, :, Q + 1 : Q + 2].astype(f32) + recv_b[k, :, Q + 2 : Q + 3].astype(f32)
        )
    unpack(slot_sum / slot_total)
    slot_in = x16[...]
    root_mean = jnp.sqrt(jnp.mean(slot_in * slot_in, axis=1, keepdims=True) + 1e-06)
    normed_v = slot_in / root_mean
    normed[...] = normed_v
    normed_b = normed_v.astype(bf16)

    loads[1].wait()
    loads[2].wait()
    row_h = lax.broadcasted_iota(jnp.int32, (16, H), 0)
    row_d = lax.broadcasted_iota(jnp.int32, (16, D), 0)
    pre_act = jnp.zeros((16, H), f32)
    for s in range(OWN):
        pre_act = jnp.where(row_h == s, nn(normed_b, expand[s]), pre_act)
    act_value, gelu_slope = gelu_pair(pre_act)
    act_b = act_value.astype(bf16)
    slot_out = jnp.zeros((16, D), f32)
    for s in range(OWN):
        slot_out = jnp.where(row_d == s, nn(act_b, reduce_[s]), slot_out)
    out_msg[...] = pack(slot_out).astype(bf16)

    gather_start(out_msg, gath_o, send_o, recv_o)
    for dz in range(4):
        zz = gather_pass(gath_o, recv_o, csend_o, crecv_o, dz)
        gather_settle(gath_o, 0, zz, every_out)
    for k in range(4):
        wait_bytes(gath_o.at[1, pl.ds(k * 16, 16)], crecv_o.at[k])
        gather_settle(gath_o, 1, k, every_out)

    loads[3].wait()
    loss_own[...] = jnp.zeros((8, 128), f32)
    for n in range(2):
        cols = slice(768 * n, 768 * n + 768)
        result = nn(comb_b[...], every_out[:, cols])
        mixed[:, cols] = result.astype(bf16)
        misfit = result - teacher[:, cols].astype(f32)
        loss_own[...] += jnp.sum(misfit * misfit)
        grad_v = (misfit / D).astype(bf16)
        grad_rows[:, cols] = grad_v
        out_part = tn(comb_b[...], grad_v)
        half[:, cols] = out_part[:HALF]
        cross_send[n] = out_part[HALF:].astype(bf16)
        pltpu.make_async_remote_copy(
            cross_send.at[n], cross_recv.at[n], csend_d.at[n], crecv_d.at[n],
            device_id=other, device_id_type=MESH,
        ).start()
    mixed_copy = pltpu.make_async_copy(mixed, mixed_h, mixed_sem)
    mixed_copy.start()
    loss_copy = pltpu.make_async_remote_copy(
        loss_own, loss_other, csend_l, crecv_l, device_id=other, device_id_type=MESH
    )
    loss_copy.start()

    def fold(cross, sem):
        for n in range(2):
            wait_bytes(cross.at[n], sem.at[n])
            cols = slice(768 * n, 768 * n + 768)
            half[:, cols] += cross[n].astype(f32)

    fold(cross_recv, crecv_d)
    for k in range(4):
        to_stack(half[64 * k : 64 * k + 64, :])
        msg_d[16 * k : 16 * k + 16] = spread(stack, Q)
    all_start(msg_d, recv_d, send_d, rsem_d)

    dcomb = nt(grad_rows[...], every_out[...])
    weighted_d = comb[...] * dcomb
    dscore = (weighted_d - comb[...] * jnp.sum(weighted_d, axis=1, keepdims=True)).astype(bf16)
    for n in range(2):
        cols = slice(768 * n, 768 * n + 768)
        key_part = tn(dscore, local[:, cols])
        half[:, cols] = key_part[:HALF]
        cross_send2[n] = key_part[HALF:].astype(bf16)
        pltpu.make_async_remote_copy(
            cross_send2.at[n], cross_recv2.at[n], csend_e.at[n], crecv_e.at[n],
            device_id=other, device_id_type=MESH,
        ).start()
    fold(cross_recv2, crecv_e)
    loss_copy.wait()
    chip_loss = loss_own[0:1, 0:1] + loss_other[0:1, 0:1]
    loss_hi = chip_loss.astype(bf16).astype(f32)
    loss_mid = (chip_loss - loss_hi).astype(bf16).astype(f32)
    extra_l = jnp.where(
        lane == 0, loss_hi, jnp.where(lane == 1, loss_mid, jnp.where(lane == 2, chip_loss - loss_hi - loss_mid, 0.0))
    )
    for j in range(4):
        stack[64 * j : 64 * j + 64, Q:] = extra_l.astype(bf16)
    for k in range(4):
        to_stack(half[64 * k : 64 * k + 64, :])
        msg_e[16 * k : 16 * k + 16] = spread(stack, Q + EXT)
    all_start(msg_e, recv_e, send_e, rsem_e)

    wait_bytes(recv_d, rsem_d)
    unpack(gather_sum(recv_d, 64))
    out_grad = x16[...].astype(bf16)
    dact = jnp.zeros((16, H), f32)
    for s in range(OWN):
        dact = jnp.where(row_h == s, nt(out_grad, reduce_[s]), dact)
    dpre = (dact * gelu_slope).astype(bf16)
    dnormed = jnp.zeros((16, D), f32)
    for s in range(OWN):
        dnormed = jnp.where(row_d == s, nt(dpre, expand[s]), dnormed)
    normed_v = normed[...]
    dslot = (dnormed - normed_v * jnp.mean(dnormed * normed_v, axis=1, keepdims=True)) / root_mean
    f_msg[:, :Q] = (pack(dslot) / slot_total).astype(bf16)
    f_msg[:, Q:] = jnp.broadcast_to(best, (16, EXT)).astype(bf16)
    tok_start(lambda k: f_msg, recv_f, send_f, rsem_f)

    wait_bytes(recv_f, rsem_f)
    back = nn(perm[...], recv_f[...].reshape(256, Q + EXT))
    for j in range(4):
        group_keys[:, Q * j : Q * j + Q] = back[64 * j : 64 * j + 64, :Q].astype(bf16)
    factor = jnp.exp(top - back[0:64, Q : Q + 1])

    @pl.loop(0, ROWS // CHUNK)
    def _(n):
        at = pl.multiple_of(n * CHUNK, CHUNK)
        dprob = nt(group_keys[...], tokens[pl.ds(at, CHUNK), :])
        weights[:, pl.ds(at, CHUNK)] = (terms[:, pl.ds(at, CHUNK)] * factor * dprob).astype(bf16)

    column_pass()
    to_stack(partial[...])
    msg_g[...] = spread(stack, Q)
    tok_start(lambda k: msg_g.at[k], recv_g, send_g, rsem_g)

    wait_bytes(recv_e, rsem_e)
    key_comb = gather_sum(recv_e, 64)
    loss_total = key_comb[0:1, Q : Q + 1] + key_comb[0:1, Q + 1 : Q + 2] + key_comb[0:1, Q + 2 : Q + 3]
    loss_o[...] = jnp.broadcast_to(loss_total / (2.0 * 16 * ROWS * D), (8, 128))
    wait_bytes(recv_g, rsem_g)
    key_disp = gather_sum(recv_g, 16)
    unpack((key_comb[:, :Q] + key_disp) / D**0.5)
    grad_o[...] = x16[0:4, :]

    gather_end(gath_k, send_k, csend_k)
    gather_end(gath_o, send_o, csend_o)
    wait_bytes(msg_b.at[pl.ds(0, 15)], send_b)
    wait_bytes(recv_f.at[pl.ds(0, 15)], send_f)
    wait_bytes(msg_g.at[pl.ds(0, 15)], send_g)
    wait_bytes(msg_d.at[pl.ds(0, 63)], send_d)
    wait_bytes(msg_e.at[pl.ds(0, 63)], send_e)
    for n in range(2):
        wait_bytes(cross_send.at[n], csend_d.at[n])
        wait_bytes(cross_send2.at[n], csend_e.at[n])
    mixed_copy.wait()


def body(tokens, dispatch_keys, expand_weight, reduce_weight, teacher):
    any_spec = pl.BlockSpec(memory_space=pl.ANY)
    vmem_spec = pl.BlockSpec(memory_space=pltpu.VMEM)
    V = pltpu.VMEM
    dma = pltpu.SemaphoreType.DMA
    mixed, loss, grad = pl.pallas_call(
        kernel,
        out_shape=(
            jax.ShapeDtypeStruct((PART, D), bf16),
            jax.ShapeDtypeStruct((8, 128), f32),
            jax.ShapeDtypeStruct((OWN, D), f32),
        ),
        in_specs=[any_spec, vmem_spec, any_spec, any_spec, any_spec],
        out_specs=(any_spec, vmem_spec, vmem_spec),
        scratch_shapes=[
            V((ROWS, D), bf16), V((OWN, D, H), bf16), V((OWN, H, D), bf16), V((PART, D), bf16),
            V((256, 256), bf16), V((256, 256), bf16), V((256, Q + EXT), bf16), V((16, Q + EXT), f32),
            V((16, Q), bf16), V((2, 64, 16, Q), bf16), V((512, D), bf16), V((64, D), bf16),
            V((64, ROWS), f32), V((64, ROWS), bf16), V((64, D), f32), V((16, 16, Q + EXT), bf16), V((16, 16, Q + EXT), bf16),
            V((16, D), f32), V((16, D), f32), V((16, Q), bf16), V((2, 64, 16, Q), bf16), V((512, D), bf16),
            V((PART, 512), f32), V((PART, 512), bf16), V((PART, D), bf16), V((PART, D), bf16),
            V((HALF, D), f32), V((2, HALF, 768), bf16), V((2, HALF, 768), bf16), V((64, 16, Q), bf16), V((64, 16, Q), bf16),
            V((2, HALF, 768), bf16), V((2, HALF, 768), bf16), V((64, 16, Q + EXT), bf16), V((64, 16, Q + EXT), bf16),
            V((8, 128), f32), V((8, 128), f32),
            V((16, Q + EXT), bf16), V((16, 16, Q + EXT), bf16), V((16, 16, Q), bf16), V((16, 16, Q), bf16),
            dma((4,)), dma, dma, dma((4,)), dma((4,)), dma((4,)), dma, dma,
            dma, dma((4,)), dma((4,)), dma((4,)), dma((2,)), dma((2,)), dma, dma,
            dma((2,)), dma((2,)), dma, dma, dma, dma,
            dma, dma, dma, dma,
        ],
        compiler_params=pltpu.CompilerParams(
            collective_id=0, has_side_effects=True, vmem_limit_bytes=60 * 2**20
        ),
    )(tokens, dispatch_keys, expand_weight, reduce_weight, teacher)
    return mixed, loss[0, 0], grad


def solution(mesh):
    in_specs = (
        P("tok", None),
        P(("tok", "exp"), None),
        P(("tok", "exp"), None, None),
        P(("tok", "exp"), None, None),
        P(("tok", "exp"), None),
    )
    out_specs = (P(("tok", "exp"), None), P(), P(("tok", "exp"), None))
    return jax.shard_map(body, mesh=mesh, in_specs=in_specs, out_specs=out_specs, check_vma=False)
```

time: 652 us -> 96.3 us (0.15)
  waiting for transfers between devices: 358 us -> 0 us
  blocking collectives: 200 us -> 0 us
  Pallas kernels: 0 us -> 90.3 us
  matrix products: 61.4 us -> 0 us
  between operations: 17.7 us -> 0.64 us
    unnamed x8 -> x0, waiting for transfers between devices: 298 us -> none
    psum x1 -> x0, blocking collectives: 99.4 us -> none  [body(): loss_total = lax.psum(jnp.sum(misfit * misfit), ('tok', 'exp'))]
    pallas_call x0 -> x1, Pallas kernels: none -> 90.3 us  [body(): pl.pallas_call(kernel, out_shape=(jax.ShapeDtypeStruct((PART, D), bf16),...]
    dot_general x12 -> x0, matrix products: 61.4 us -> none  [the longest x1 13.6 us: body(): term = jnp.dot(dlogit, tokens, preferred_element_type=jnp.float32)]
    all_gather x2 -> x0, waiting for transfers between devices: 60.1 us -> none  [the longest x1 60.1 us: body(): every_out = lax.all_gather(slot_out, ('tok', 'exp'), axis=0, tiled=True)]
    all_gather x2 -> x0, blocking collectives: 40.8 us -> none  [the longest x1 21.1 us: body(): group_scaled = lax.all_gather(scaled_b, 'tok', axis=0, tiled=True)]
    pmax x1 -> x0, blocking collectives: 30.9 us -> none  [body(): col_max = lax.pmax(jnp.max(logits, axis=1), 'tok')]
    unnamed x1 -> x0, blocking collectives: 28.7 us -> none
  transfers between devices with their start and end apart: 5 -> 0, of which waited for: 4 -> 0; matrix products, arithmetic and copies ran while one was open for 4% -> 0% of each run, Pallas kernels for 0% -> 0%
where the time goes in v1:
time: 96.3 us; the launch traced here: 95.9 us
  Pallas kernels  90.3 us (94%)
  local copies, waits for them, and re-layouts  5.03 us (5%)
    pallas_call x1, Pallas kernels, body(): pl.pallas_call(kernel, out_shape=(jax.ShapeDtypeStruct((PART, D), bf16),...  90.3 us
    unnamed x2, local copies, waits for them, and re-layouts  3.85 us

profile of v1, /device:TPU:1, one launch (start us, length us, event | category | flops | bytes accessed | tf_op | source)
XLA Modules:
  0.0 95.9 jit_solution(10337198730541896295)
XLA Ops:
  0.6 90.3 %shard_map.76 = (bf16[448,1536]{1,0:T(8,128)(2,1)}, f32[8,128]{1,0:T(8,128)}, f32[4,1536]{1,0:T(4,128)}) custom-call(bf16[3584,1536]{1,0:T(8,128)(2,1)} %tokens_h.1, bf16[4,1536]{1,0:T(4,128)(2,1)} %keys.1, bf16[4,1536,512]{2,1,0:T(8,128)(2,1)} %expand_h.1, bf16[4,512,1536]{2,1,0:T(8,128)(2,1)} %reduce_h.1, bf16[448,1536]{1,0:T(8,128)(2,1)} %teacher_h.1), custom_call_target="tpu_custom_call" | custom-call | tf_op jit(solution)/shard_map/pallas_call | solution.py:402
  90.9 1.2 %slice.3 = f32[1,1]{1,0:T(1,128)} slice(f32[8,128]{1,0:T(8,128)} %get-tuple-element.7), slice={[0:1], [0:1]} | slice | bytes 8 | tf_op jit(solution)/shard_map/slice | solution.py:431
  92.1 2.5 %copy.10 = bf16[448,1536]{1,0:T(8,128)(2,1)} copy(bf16[448,1536]{1,0:T(8,128)(2,1)} %get-tuple-element.12) | data formatting | bytes 2752512
  94.6 1.3 %copy.11 = f32[4,1536]{1,0:T(4,128)} copy(f32[4,1536]{1,0:T(4,128)} %get-tuple-element.14) | data formatting | bytes 49152

commit v2 on v0

v2 whole, which is shorter than its diff:
```python
import functools
import jax
import jax.numpy as jnp
from jax import lax
from jax.experimental import pallas as pl
from jax.experimental.pallas import tpu as pltpu
from jax.sharding import PartitionSpec as P

MESH = pl.DeviceIdType.MESH
f32, bf16 = jnp.float32, jnp.bfloat16
D, H, ROWS, PART, OWN, GROUP, HALF = 1536, 512, 3584, 448, 4, 64, 256
TOK = 16
PARTS = 3
WIDE = 512
LANES = 128
Q = PARTS * LANES
CHUNK = 1792
gelu_coef = 0.7978845608028654
cube_coef = 0.044715


def gelu_pair(values):
    tanh_value = jnp.tanh(gelu_coef * (values + cube_coef * values * values * values))
    output = 0.5 * values * (1.0 + tanh_value)
    derivative = 0.5 * (1.0 + tanh_value) + 0.5 * values * (
        1.0 - tanh_value * tanh_value
    ) * gelu_coef * (1.0 + 3.0 * cube_coef * values * values)
    return (output, derivative)


def nn(a, b):
    return lax.dot_general(a, b, (((1,), (0,)), ((), ())), preferred_element_type=f32)


def nt(a, b):
    return lax.dot_general(a, b, (((1,), (1,)), ((), ())), preferred_element_type=f32)


def tn(a, b):
    return lax.dot_general(a, b, (((0,), (0,)), ((), ())), preferred_element_type=f32)


def wait_bytes(ref, sem):
    pltpu.make_async_copy(ref, ref, sem).wait()


class Pending:
    def __init__(self):
        self.open = {}

    def add(self, name, ref, sem):
        self.open[name] = (ref, sem)

    def wait(self, name):
        wait_bytes(*self.open.pop(name))

    def finish(self):
        for name in list(self.open):
            self.wait(name)


def kernel(
    tokens_h, keys, expand_h, reduce_h, teacher_h,
    mixed_h, loss_o, grad_o,
    tokens, expand, reduce_, teacher, perm, perm_t, wide,
    key_msg, recv_k, all_keys,
    terms, weights, msg_b, recv_b,
    normed, x16, out_msg, gath_o, every_out,
    comb, comb_b, grad_rows, mixed,
    half_d, cross_d, arrived_d, msg_d, recv_d,
    half_e, cross_e, arrived_e, fold_e, recv_e, loss_own, loss_other, loss_z,
    msg_f, recv_f, msg_g, recv_g,
    load_sem, mixed_sem, ssem_k, rsem_k, ssem_kz, rsem_kz, csend_k, crecv_k,
    ssem_b, rsem_b, ssem_o, rsem_o, csend_o, crecv_o,
    csend_d, crecv_d, ssem_d, rsem_d, csend_e, crecv_e, ssem_e, rsem_e,
    csend_l, crecv_l, ssem_l, rsem_l, ssem_f, rsem_f, ssem_g, rsem_g,
):
    t = lax.axis_index("tok")
    e = lax.axis_index("exp")
    x, y = t >> 2, t & 3
    z, c = e >> 1, e & 1
    other = (t, z * 2 + 1 - c)
    flying = Pending()
    finish = flying.finish

    for n, (name, src, dst) in enumerate((
        ("tokens", tokens_h, tokens), ("expand", expand_h, expand),
        ("reduce", reduce_h, reduce_), ("teacher", teacher_h, teacher),
    )):
        pltpu.make_async_copy(src, dst, load_sem.at[n]).start()
        flying.add(name, dst, load_sem.at[n])

    def peer(k):
        t2 = ((x + ((k >> 2) & 3)) & 3) * 4 + ((y + (k & 3)) & 3)
        return t2, (z + (k >> 4)) & 3

    barrier = pltpu.get_barrier_semaphore()

    def greet(k, carry):
        t2, z2 = peer(k)
        pl.semaphore_signal(barrier, inc=1, device_id=(t2, z2 * 2 + c), device_id_type=MESH)
        return carry

    lax.fori_loop(1, 64, greet, 0)
    pl.semaphore_signal(barrier, inc=1, device_id=other, device_id_type=MESH)

    row = lax.broadcasted_iota(jnp.int32, (256, 256), 0)
    col = lax.broadcasted_iota(jnp.int32, (256, 256), 1)

    def moved(r):
        return ((r >> 2) & 15) * 16 + (r >> 6) * 4 + (r & 3)

    perm[...] = jnp.where(col == moved(row), 1.0, 0.0).astype(bf16)
    perm_t[...] = jnp.where(row == moved(col), 1.0, 0.0).astype(bf16)

    def place(n, j):
        return slice(WIDE * n + LANES * j, WIDE * n + LANES * j + LANES)

    def span(n, width=LANES):
        return slice(width * n, width * n + width)

    def pack(value):
        for n in range(PARTS):
            for j in range(4):
                wide[4 * j : 4 * j + 4, span(n)] = value[0:4, place(n, j)]
        return wide[...]

    def unpack(message, n):
        wide[:, span(n)] = message
        for j in range(4):
            x16[0:4, place(n, j)] = wide[4 * j : 4 * j + 4, span(n)]

    def lines(value):
        return jnp.concatenate([value[:, span(j)] for j in range(4)], axis=0).astype(bf16)

    def spread(stacked):
        return nn(perm_t[...], stacked).astype(bf16)

    def remote(src, dst, send, recv, device):
        pltpu.make_async_remote_copy(
            src, dst, send, recv, device_id=device, device_id_type=MESH
        ).start()

    def cross(name, src, dst, send, recv):
        remote(src, dst, send, recv, other)
        flying.add(name + "_out", src, send)
        flying.add(name + "_in", dst, recv)

    def to_tok(name, src_of, recv_ref, send, recv):
        pltpu.make_async_copy(src_of(t), recv_ref.at[t], recv).start()

        def step(k, carry):
            t2, _ = peer(k)
            remote(src_of(t2), recv_ref.at[t], send, recv, (t2, e))
            return carry

        lax.fori_loop(1, TOK, step, 0)
        flying.add(name + "_out", recv_ref.at[pl.ds(0, TOK - 1)], send)
        flying.add(name + "_in", recv_ref, recv)

    def to_all(name, src_of, recv_ref, send, recv):
        me = z * TOK + t
        pltpu.make_async_copy(src_of(me), recv_ref.at[me], recv).start()

        def step(k, carry):
            t2, z2 = peer(k)
            remote(src_of(z2 * TOK + t2), recv_ref.at[me], send, recv, (t2, z2 * 2 + c))
            return carry

        lax.fori_loop(1, 64, step, 0)
        flying.add(name + "_out", recv_ref.at[pl.ds(0, 63)], send)
        flying.add(name + "_in", recv_ref, recv)

    def to_z(name, src_of, dst, send, recv, three):
        for dz in range(1, 4):
            z2 = (z + dz) & 3
            remote(src_of(z2), dst, send, recv, (t, z2 * 2 + c))
        flying.add(name + "_out", three, send)

    def sum_of(ref, count):
        return lax.fori_loop(
            0, count, lambda k, s: s + ref[k].astype(f32), jnp.zeros(ref.shape[1:], f32)
        )

    x16[...] = jnp.zeros((16, D), f32)
    key_msg[...] = pack(keys[...].astype(f32)).astype(bf16)
    pl.semaphore_wait(barrier, 64)

    to_tok("keys", lambda k: key_msg, recv_k, ssem_k, rsem_k)
    flying.wait("keys_in")
    mine = pl.ds(pl.multiple_of(z * GROUP, GROUP), GROUP)
    moved_k = nn(perm[...], recv_k[...].reshape(256, Q)).astype(bf16)
    for n in range(PARTS):
        for j in range(4):
            all_keys[mine, place(n, j)] = moved_k[64 * j : 64 * j + 64, span(n)]

    def key_rows(half, dz):
        return pl.ds(pl.multiple_of(half * HALF + ((z + dz) & 3) * GROUP, GROUP), GROUP)

    def key_cross(dz):
        zz = (z + dz) & 3
        cross(
            f"keys_cross{dz}", all_keys.at[key_rows(0, dz)], all_keys.at[key_rows(1, dz)],
            csend_k.at[zz], crecv_k.at[zz],
        )

    to_z(
        "keys_z", lambda z2: all_keys.at[mine], all_keys.at[mine], ssem_kz, rsem_kz.at[z],
        all_keys.at[pl.ds(0, 3 * GROUP)],
    )
    for dz in range(1, 4):
        flying.add(f"keys_z{dz}", all_keys.at[key_rows(0, dz)], rsem_kz.at[(z + dz) & 3])
    key_cross(0)
    flying.wait("tokens")

    @pl.loop(0, ROWS // CHUNK)
    def _(n):
        at = pl.multiple_of(n * CHUNK, CHUNK)
        terms[:, pl.ds(at, CHUNK)] = nt(all_keys[mine, :], tokens[pl.ds(at, CHUNK), :])

    top = jnp.max(terms[...], axis=1, keepdims=True).astype(bf16).astype(f32)
    exp_terms = jnp.exp(terms[...] - top)
    terms[...] = exp_terms
    weights[...] = exp_terms.astype(bf16)
    total = jnp.sum(exp_terms, axis=1, keepdims=True)
    lane = lax.broadcasted_iota(jnp.int32, (GROUP, LANES), 1)
    total_hi = total.astype(bf16).astype(f32)
    extra = jnp.where(
        lane == 0, top, jnp.where(lane == 1, total_hi, jnp.where(lane == 2, total - total_hi, 0.0))
    )
    extra_b = extra.astype(bf16)
    msg_b[PARTS] = spread(jnp.concatenate([extra_b] * 4, axis=0)).reshape(TOK, 16, LANES)
    to_tok("b3", lambda k: msg_b.at[PARTS, k], recv_b.at[PARTS], ssem_b.at[PARTS], rsem_b.at[PARTS])
    for n in range(PARTS):
        part = nn(weights[...], tokens[:, span(n, WIDE)])
        msg_b[n] = spread(lines(part)).reshape(TOK, 16, LANES)
        to_tok(f"b{n}", lambda k: msg_b.at[n, k], recv_b.at[n], ssem_b.at[n], rsem_b.at[n])

    for dz in range(1, 4):
        flying.wait(f"keys_z{dz}")
        key_cross(dz)
    for dz in range(4):
        flying.wait(f"keys_cross{dz}_in")
    local = tokens.at[pl.ds(pl.multiple_of(e * PART, GROUP), PART)]
    scores = nt(local[...], all_keys[...])
    row_terms = jnp.exp(scores - jnp.max(scores, axis=1, keepdims=True))
    comb_v = row_terms / jnp.sum(row_terms, axis=1, keepdims=True)
    comb[...] = comb_v
    comb_b[...] = comb_v.astype(bf16)

    flying.wait("b3_in")
    best = recv_b[PARTS, 0, :, 0:1].astype(f32)
    for k in range(1, TOK):
        best = jnp.maximum(best, recv_b[PARTS, k, :, 0:1].astype(f32))
    scales = []
    slot_total = jnp.zeros((16, 1), f32)
    for k in range(TOK):
        held = recv_b[PARTS, k].astype(f32)
        scales.append(jnp.exp(held[:, 0:1] - best))
        slot_total += scales[k] * (held[:, 1:2] + held[:, 2:3])
    for n in range(PARTS):
        flying.wait(f"b{n}_in")
        slot_sum = jnp.zeros((16, LANES), f32)
        for k in range(TOK):
            slot_sum += scales[k] * recv_b[n, k].astype(f32)
        unpack(slot_sum / slot_total, n)
    slot_in = x16[...]
    root_mean = jnp.sqrt(jnp.mean(slot_in * slot_in, axis=1, keepdims=True) + 1e-06)
    normed_v = slot_in / root_mean
    normed[...] = normed_v
    normed_b = normed_v.astype(bf16)

    flying.wait("expand")
    flying.wait("reduce")
    row_h = lax.broadcasted_iota(jnp.int32, (16, H), 0)
    row_d = lax.broadcasted_iota(jnp.int32, (16, D), 0)
    pre_act = jnp.zeros((16, H), f32)
    for s in range(OWN):
        pre_act = jnp.where(row_h == s, nn(normed_b, expand[s]), pre_act)
    act_value, gelu_slope = gelu_pair(pre_act)
    act_b = act_value.astype(bf16)
    slot_out = jnp.zeros((16, D), f32)
    for s in range(OWN):
        slot_out = jnp.where(row_d == s, nn(act_b, reduce_[s]), slot_out)
    packed_out = pack(slot_out).astype(bf16)
    for n in range(PARTS):
        out_msg[n] = packed_out[:, span(n)]
    for n in range(PARTS):
        to_all(f"o{n}", lambda k: out_msg.at[n], gath_o.at[n, 0], ssem_o.at[n], rsem_o.at[n])

    flying.wait("teacher")

    def settle(n, half):
        block = jnp.concatenate(
            [gath_o[n, half, span(g, TOK)].reshape(256, LANES) for g in range(4)], axis=1
        )
        r = nn(perm[...], block).astype(bf16)
        for g in range(4):
            for j in range(4):
                every_out[half * HALF + g * GROUP : half * HALF + (g + 1) * GROUP, place(n, j)] = r[
                    64 * j : 64 * j + 64, span(g)
                ]

    def pass_on(n):
        flying.wait(f"o{n}_in")
        cross(f"o_cross{n}", gath_o.at[n, 0], gath_o.at[n, 1], csend_o.at[n], crecv_o.at[n])
        settle(n, 0)

    def combine(n):
        flying.wait(f"o_cross{n}_in")
        settle(n, 1)
        cols = span(n, WIDE)
        result = nn(comb_b[...], every_out[:, cols])
        mixed[:, cols] = result.astype(bf16)
        misfit = result - teacher[:, cols].astype(f32)
        grad_v = (misfit / D).astype(bf16)
        grad_rows[:, cols] = grad_v
        out_part = tn(comb_b[...], grad_v)
        half_d[:, cols] = out_part[:HALF]
        cross_d[n] = out_part[HALF:].astype(bf16)
        cross(f"d_cross{n}", cross_d.at[n], arrived_d.at[n], csend_d.at[n], crecv_d.at[n])
        return jnp.sum(misfit * misfit)

    def send_d(n):
        flying.wait(f"d_cross{n}_in")
        whole = half_d[:, span(n, WIDE)] + arrived_d[n].astype(f32)
        stacked = jnp.concatenate([lines(whole[span(g, GROUP)]) for g in range(4)], axis=1)
        r = spread(stacked)
        for g in range(4):
            msg_d[n, span(g, TOK)] = r[:, span(g)].reshape(TOK, 16, LANES)
        to_all(f"d{n}", lambda k: msg_d.at[n, k], recv_d.at[n], ssem_d.at[n], rsem_d.at[n])

    pass_on(0)
    loss_sum = combine(0)
    pass_on(1)
    send_d(0)
    loss_sum += combine(1)
    pass_on(2)
    send_d(1)
    loss_sum += combine(2)
    loss_own[...] = jnp.full((8, LANES), loss_sum, f32)
    cross("loss", loss_own, loss_other, csend_l, crecv_l)
    send_d(2)
    pltpu.make_async_copy(mixed, mixed_h, mixed_sem).start()
    flying.add("mixed", mixed, mixed_sem)

    dcomb = nt(grad_rows[...], every_out[...])
    weighted_d = comb[...] * dcomb
    dscore = (weighted_d - comb[...] * jnp.sum(weighted_d, axis=1, keepdims=True)).astype(bf16)
    for n in range(PARTS):
        key_part = tn(dscore, local[:, span(n, WIDE)])
        half_e[:, span(n, WIDE)] = key_part[:HALF]
        cross_e[n] = key_part[HALF:].astype(bf16)
        cross(f"e_cross{n}", cross_e.at[n], arrived_e.at[n], csend_e.at[n], crecv_e.at[n])
    flying.wait("loss_in")
    loss_z[z] = loss_own[...] + loss_other[...]
    to_z("loss_z", lambda z2: loss_z.at[z], loss_z.at[z], ssem_l, rsem_l.at[z], loss_z.at[pl.ds(0, 3)])
    for dz in range(1, 4):
        flying.add(f"loss_z{dz}", loss_z.at[(z + dz) & 3], rsem_l.at[(z + dz) & 3])
    for n in range(PARTS):
        flying.wait(f"e_cross{n}_in")
        whole_e = (half_e[:, span(n, WIDE)] + arrived_e[n].astype(f32)).astype(bf16)
        for g in range(4):
            fold_e[g, :, span(n, WIDE)] = whole_e[span(g, GROUP)]

    dact = jnp.zeros((16, H), f32)
    for n in range(PARTS):
        flying.wait(f"d{n}_in")
        unpack(sum_of(recv_d.at[n], 64), n)
        cols = span(n, WIDE)
        out_grad = x16[:, cols].astype(bf16)
        for s in range(OWN):
            dact = jnp.where(row_h == s, dact + nt(out_grad, reduce_[s, :, cols]), dact)
    to_z("e", lambda z2: fold_e.at[z2], recv_e.at[z], ssem_e, rsem_e, fold_e.at[pl.ds(0, 3)])
    pltpu.make_async_copy(fold_e.at[z], recv_e.at[z], rsem_e).start()
    flying.add("e_in", recv_e, rsem_e)
    dpre = (dact * gelu_slope).astype(bf16)
    dnormed = jnp.zeros((16, D), f32)
    for s in range(OWN):
        dnormed = jnp.where(row_d == s, nt(dpre, expand[s]), dnormed)
    normed_v = normed[...]
    dslot = (dnormed - normed_v * jnp.mean(dnormed * normed_v, axis=1, keepdims=True)) / root_mean
    msg_f[:, :Q] = (pack(dslot) / slot_total).astype(bf16)
    for dz in range(1, 4):
        flying.wait(f"loss_z{dz}")
    loss_line = ((loss_z[0] + loss_z[1]) + (loss_z[2] + loss_z[3]))[0:1, 0:1]
    loss_hi = loss_line.astype(bf16).astype(f32)
    loss_mid = (loss_line - loss_hi).astype(bf16).astype(f32)
    lane_f = lax.broadcasted_iota(jnp.int32, (16, LANES), 1)
    extra_f = jnp.where(lane_f == 0, best, 0.0)
    for n, value in enumerate((loss_hi, loss_mid, loss_line - loss_hi - loss_mid)):
        extra_f = jnp.where(lane_f == n + 1, value, extra_f)
    msg_f[:, Q:] = extra_f.astype(bf16)
    to_tok("f", lambda k: msg_f, recv_f, ssem_f, rsem_f)

    flying.wait("f_in")
    flying.wait("keys_z_out")
    for dz in range(4):
        flying.wait(f"keys_cross{dz}_out")
    back = nn(perm[...], recv_f[...].reshape(256, Q + LANES))
    for n in range(PARTS):
        for j in range(4):
            all_keys[0:GROUP, place(n, j)] = back[64 * j : 64 * j + 64, span(n)].astype(bf16)
    factor = jnp.exp(top - back[0:GROUP, Q : Q + 1])
    losses = jnp.sum(back[0:GROUP, Q + 1 : Q + 4], axis=(0, 1), keepdims=True) / OWN
    loss_o[...] = losses / (2.0 * TOK * ROWS * D)

    @pl.loop(0, ROWS // CHUNK)
    def _(n):
        at = pl.multiple_of(n * CHUNK, CHUNK)
        dprob = nt(all_keys[0:GROUP, :], tokens[pl.ds(at, CHUNK), :])
        weights[:, pl.ds(at, CHUNK)] = (terms[:, pl.ds(at, CHUNK)] * factor * dprob).astype(bf16)

    flying.wait("e_in")
    for n in range(PARTS):
        cols = span(n, WIDE)
        part = nn(weights[...], tokens[:, cols])
        for k in range(4):
            part += recv_e[k, :, cols].astype(f32)
        msg_g[n] = spread(lines(part)).reshape(TOK, 16, LANES)
        to_tok(f"g{n}", lambda k: msg_g.at[n, k], recv_g.at[n], ssem_g.at[n], rsem_g.at[n])
    for n in range(PARTS):
        flying.wait(f"g{n}_in")
        unpack(sum_of(recv_g.at[n], TOK) / D**0.5, n)
    grad_o[...] = x16[0:4, :]
    finish()


def hand_over(mixed_in, loss_in, grad_in, mixed_out, loss_out, grad_out, held, sem_in, sem_out):
    blocks = [pl.ds(n * 112, 112) for n in range(4)]
    ins = [pltpu.make_async_copy(mixed_in.at[b], held.at[b], sem_in.at[n]) for n, b in enumerate(blocks)]
    outs = [pltpu.make_async_copy(held.at[b], mixed_out.at[b], sem_out.at[n]) for n, b in enumerate(blocks)]
    for copy in ins:
        copy.start()
    loss_out[...] = loss_in[...]
    grad_out[...] = grad_in[...]
    for n in range(4):
        ins[n].wait()
        outs[n].start()
    for copy in outs:
        copy.wait()


def body(tokens, dispatch_keys, expand_weight, reduce_weight, teacher):
    any_spec = pl.BlockSpec(memory_space=pl.ANY)
    vmem_spec = pl.BlockSpec(memory_space=pltpu.VMEM)
    V = pltpu.VMEM
    dma = pltpu.SemaphoreType.DMA
    out_shape = (
        jax.ShapeDtypeStruct((PART, D), bf16),
        jax.ShapeDtypeStruct((1, 1), f32),
        jax.ShapeDtypeStruct((OWN, D), f32),
    )
    mixed, loss, grad = pl.pallas_call(
        kernel,
        out_shape=out_shape,
        in_specs=[any_spec, vmem_spec, any_spec, any_spec, any_spec],
        out_specs=(any_spec, vmem_spec, vmem_spec),
        scratch_shapes=[
            V((ROWS, D), bf16), V((OWN, D, H), bf16), V((OWN, H, D), bf16), V((PART, D), bf16),
            V((256, 256), bf16), V((256, 256), bf16), V((16, Q), f32),
            V((16, Q), bf16), V((TOK, 16, Q), bf16), V((2 * HALF, D), bf16),
            V((GROUP, ROWS), f32), V((GROUP, ROWS), bf16),
            V((PARTS + 1, TOK, 16, LANES), bf16), V((PARTS + 1, TOK, 16, LANES), bf16),
            V((16, D), f32), V((16, D), f32), V((PARTS, 16, LANES), bf16),
            V((PARTS, 2, 64, 16, LANES), bf16), V((2 * HALF, D), bf16),
            V((PART, 2 * HALF), f32), V((PART, 2 * HALF), bf16), V((PART, D), bf16), V((PART, D), bf16),
            V((HALF, D), f32), V((PARTS, HALF, WIDE), bf16), V((PARTS, HALF, WIDE), bf16),
            V((PARTS, 64, 16, LANES), bf16), V((PARTS, 64, 16, LANES), bf16),
            V((HALF, D), f32), V((PARTS, HALF, WIDE), bf16), V((PARTS, HALF, WIDE), bf16),
            V((4, GROUP, D), bf16), V((4, GROUP, D), bf16),
            V((8, LANES), f32), V((8, LANES), f32), V((4, 8, LANES), f32),
            V((16, Q + LANES), bf16), V((TOK, 16, Q + LANES), bf16),
            V((PARTS, TOK, 16, LANES), bf16), V((PARTS, TOK, 16, LANES), bf16),
            dma((4,)), dma, dma, dma, dma, dma((4,)), dma((4,)), dma((4,)),
            dma((PARTS + 1,)), dma((PARTS + 1,)), dma((PARTS,)), dma((PARTS,)), dma((PARTS,)), dma((PARTS,)),
            dma((PARTS,)), dma((PARTS,)), dma((PARTS,)), dma((PARTS,)), dma((PARTS,)), dma((PARTS,)), dma, dma,
            dma, dma, dma, dma((4,)), dma, dma, dma((PARTS,)), dma((PARTS,)),
        ],
        compiler_params=pltpu.CompilerParams(
            collective_id=0, has_side_effects=True, vmem_limit_bytes=60 * 2**20
        ),
    )(tokens, dispatch_keys, expand_weight, reduce_weight, teacher)
    mixed, loss, grad = pl.pallas_call(
        hand_over,
        out_shape=out_shape,
        in_specs=[any_spec, vmem_spec, vmem_spec],
        out_specs=(any_spec, vmem_spec, vmem_spec),
        scratch_shapes=[V((PART, D), bf16), dma((4,)), dma((4,))],
    )(mixed, loss, grad)
    return mixed, loss.reshape(()), grad


def solution(mesh):
    in_specs = (
        P("tok", None),
        P(("tok", "exp"), None),
        P(("tok", "exp"), None, None),
        P(("tok", "exp"), None, None),
        P(("tok", "exp"), None),
    )
    out_specs = (P(("tok", "exp"), None), P(), P(("tok", "exp"), None))
    return jax.shard_map(body, mesh=mesh, in_specs=in_specs, out_specs=out_specs, check_vma=False)
```

time: 652 us -> 83.7 us (0.13)
  waiting for transfers between devices: 358 us -> 0 us
  blocking collectives: 200 us -> 0 us
  Pallas kernels: 0 us -> 82.8 us
  matrix products: 61.4 us -> 0 us
  between operations: 17.7 us -> 0.64 us
  local copies, waits for them, and re-layouts: 9.23 us -> 0 us
    unnamed x8 -> x0, waiting for transfers between devices: 298 us -> none
    psum x1 -> x0, blocking collectives: 99.4 us -> none  [body(): loss_total = lax.psum(jnp.sum(misfit * misfit), ('tok', 'exp'))]
    pallas_call x0 -> x2, Pallas kernels: none -> 82.8 us  [the longest x1 78.7 us: body(): pl.pallas_call(kernel, out_shape=out_shape, in_specs=[any_spec, vmem_spec...]
    dot_general x12 -> x0, matrix products: 61.4 us -> none  [the longest x1 13.6 us: body(): term = jnp.dot(dlogit, tokens, preferred_element_type=jnp.float32)]
    all_gather x2 -> x0, waiting for transfers between devices: 60.1 us -> none  [the longest x1 60.1 us: body(): every_out = lax.all_gather(slot_out, ('tok', 'exp'), axis=0, tiled=True)]
    all_gather x2 -> x0, blocking collectives: 40.8 us -> none  [the longest x1 21.1 us: body(): group_scaled = lax.all_gather(scaled_b, 'tok', axis=0, tiled=True)]
    pmax x1 -> x0, blocking collectives: 30.9 us -> none  [body(): col_max = lax.pmax(jnp.max(logits, axis=1), 'tok')]
    unnamed x1 -> x0, blocking collectives: 28.7 us -> none
  transfers between devices with their start and end apart: 5 -> 0, of which waited for: 4 -> 0; matrix products, arithmetic and copies ran while one was open for 4% -> 0% of each run, Pallas kernels for 0% -> 0%
where the time goes in v2:
time: 83.7 us; the launch traced here: 83.5 us
  Pallas kernels  82.8 us (99%)
    pallas_call x1, Pallas kernels, body(): pl.pallas_call(kernel, out_shape=out_shape, in_specs=[any_spec, vmem_spec...  78.7 us
    pallas_call x1, Pallas kernels, body(): pl.pallas_call(hand_over, out_shape=out_shape, in_specs=[any_spec, vmem_s...  4.1 us

profile of v2, /device:TPU:1, one launch (start us, length us, event | category | flops | bytes accessed | tf_op | source)
XLA Modules:
  0.0 83.5 jit_solution(15967090117582233010)
XLA Ops:
  0.6 78.7 %shard_map.76 = (bf16[448,1536]{1,0:T(8,128)(2,1)}, f32[1,1]{1,0:T(1,128)}, f32[4,1536]{1,0:T(4,128)}) custom-call(bf16[3584,1536]{1,0:T(8,128)(2,1)} %tokens_h.1, bf16[4,1536]{1,0:T(4,128)(2,1)} %keys.1, bf16[4,1536,512]{2,1,0:T(8,128)(2,1)} %expand_h.1, bf16[4,512,1536]{2,1,0:T(8,128)(2,1)} %reduce_h.1, bf16[448,1536]{1,0:T(8,128)(2,1)} %teacher_h.1), custom_call_target="tpu_custom_call" | custom-call | tf_op jit(solution)/shard_map/pallas_call | solution.py:454
  79.4 4.1 %shard_map.77 = (bf16[448,1536]{1,0:T(8,128)(2,1)}, f32[1,1]{1,0:T(1,128)}, f32[4,1536]{1,0:T(4,128)}) custom-call(bf16[448,1536]{1,0:T(8,128)(2,1)} %get-tuple-element.9.mixed_in, f32[1,1]{1,0:T(1,128)} %get-tuple-element.10.loss_in, f32[4,1536]{1,0:T(4,128)} %get-tuple-element.11.grad_in), custom_call_target="tpu_custom_call" | custom-call | tf_op jit(solution)/shard_map/pallas_call | solution.py:484

commit v3 on v2

--- a/solution.py
+++ b/solution.py
@@ -83,6 +83,26 @@
     flying = Pending()
     finish = flying.finish
 
+    def offset(d):
+        return 2 - 2 * (d & 1) + ((d + (d >> 1)) & 1)
+
+    def peer(k):
+        t2 = ((x + offset((k >> 2) & 3)) & 3) * 4 + ((y + offset(k & 3)) & 3)
+        return t2, (z + offset(k >> 4)) & 3
+
+    def peer_tok(k):
+        return peer(k + 48)[0]
+
+    barrier = pltpu.get_barrier_semaphore()
+
+    def greet(k, carry):
+        t2, z2 = peer(k)
+        pl.semaphore_signal(barrier, inc=1, device_id=(t2, z2 * 2 + c), device_id_type=MESH)
+        return carry
+
+    lax.fori_loop(0, 63, greet, 0)
+    pl.semaphore_signal(barrier, inc=1, device_id=other, device_id_type=MESH)
+
     for n, (name, src, dst) in enumerate((
         ("tokens", tokens_h, tokens), ("expand", expand_h, expand),
         ("reduce", reduce_h, reduce_), ("teacher", teacher_h, teacher),
@@ -90,20 +110,6 @@
         pltpu.make_async_copy(src, dst, load_sem.at[n]).start()
         flying.add(name, dst, load_sem.at[n])
 
-    def peer(k):
-        t2 = ((x + ((k >> 2) & 3)) & 3) * 4 + ((y + (k & 3)) & 3)
-        return t2, (z + (k >> 4)) & 3
-
-    barrier = pltpu.get_barrier_semaphore()
-
-    def greet(k, carry):
-        t2, z2 = peer(k)
-        pl.semaphore_signal(barrier, inc=1, device_id=(t2, z2 * 2 + c), device_id_type=MESH)
-        return carry
-
-    lax.fori_loop(1, 64, greet, 0)
-    pl.semaphore_signal(barrier, inc=1, device_id=other, device_id_type=MESH)
-
     row = lax.broadcasted_iota(jnp.int32, (256, 256), 0)
     col = lax.broadcasted_iota(jnp.int32, (256, 256), 1)
 
@@ -150,11 +156,11 @@
         pltpu.make_async_copy(src_of(t), recv_ref.at[t], recv).start()
 
         def step(k, carry):
-            t2, _ = peer(k)
+            t2 = peer_tok(k)
             remote(src_of(t2), recv_ref.at[t], send, recv, (t2, e))
             return carry
 
-        lax.fori_loop(1, TOK, step, 0)
+        lax.fori_loop(0, TOK - 1, step, 0)
         flying.add(name + "_out", recv_ref.at[pl.ds(0, TOK - 1)], send)
         flying.add(name + "_in", recv_ref, recv)
 
@@ -167,7 +173,7 @@
             remote(src_of(z2 * TOK + t2), recv_ref.at[me], send, recv, (t2, z2 * 2 + c))
             return carry
 
-        lax.fori_loop(1, 64, step, 0)
+        lax.fori_loop(0, 63, step, 0)
         flying.add(name + "_out", recv_ref.at[pl.ds(0, 63)], send)
         flying.add(name + "_in", recv_ref, recv)
 
@@ -362,6 +368,9 @@
         whole_e = (half_e[:, span(n, WIDE)] + arrived_e[n].astype(f32)).astype(bf16)
         for g in range(4):
             fold_e[g, :, span(n, WIDE)] = whole_e[span(g, GROUP)]
+    to_z("e", lambda z2: fold_e.at[z2], recv_e.at[z], ssem_e, rsem_e, fold_e.at[pl.ds(0, 3)])
+    pltpu.make_async_copy(fold_e.at[z], recv_e.at[z], rsem_e).start()
+    flying.add("e_in", recv_e, rsem_e)
 
     dact = jnp.zeros((16, H), f32)
     for n in range(PARTS):
@@ -371,9 +380,6 @@
         out_grad = x16[:, cols].astype(bf16)
         for s in range(OWN):
             dact = jnp.where(row_h == s, dact + nt(out_grad, reduce_[s, :, cols]), dact)
-    to_z("e", lambda z2: fold_e.at[z2], recv_e.at[z], ssem_e, rsem_e, fold_e.at[pl.ds(0, 3)])
-    pltpu.make_async_copy(fold_e.at[z], recv_e.at[z], rsem_e).start()
-    flying.add("e_in", recv_e, rsem_e)
     dpre = (dact * gelu_slope).astype(bf16)
     dnormed = jnp.zeros((16, D), f32)
     for s in range(OWN):
@@ -426,18 +432,19 @@
     finish()
 
 
-def hand_over(mixed_in, loss_in, grad_in, mixed_out, loss_out, grad_out, held, sem_in, sem_out):
-    blocks = [pl.ds(n * 112, 112) for n in range(4)]
-    ins = [pltpu.make_async_copy(mixed_in.at[b], held.at[b], sem_in.at[n]) for n, b in enumerate(blocks)]
-    outs = [pltpu.make_async_copy(held.at[b], mixed_out.at[b], sem_out.at[n]) for n, b in enumerate(blocks)]
-    for copy in ins:
+def hand_over(*refs):
+    ins, outs, held, (sem_in, sem_out) = refs[:3], refs[3:6], refs[6:9], refs[9:]
+    rows = [pl.ds(n * 112, 112) for n in range(4)]
+    steps = [(ins[k], held[k], outs[k]) for k in (1, 2)]
+    steps += [tuple(r.at[b] for r in (ins[0], held[0], outs[0])) for b in rows]
+    first = [pltpu.make_async_copy(a, b, sem_in.at[n]) for n, (a, b, _) in enumerate(steps)]
+    second = [pltpu.make_async_copy(b, c, sem_out.at[n]) for n, (_, b, c) in enumerate(steps)]
+    for copy in first:
         copy.start()
-    loss_out[...] = loss_in[...]
-    grad_out[...] = grad_in[...]
-    for n in range(4):
-        ins[n].wait()
-        outs[n].start()
-    for copy in outs:
+    for n in range(len(steps)):
+        first[n].wait()
+        second[n].start()
+    for copy in second:
         copy.wait()
 
 
@@ -478,15 +485,15 @@
             dma, dma, dma, dma((4,)), dma, dma, dma((PARTS,)), dma((PARTS,)),
         ],
         compiler_params=pltpu.CompilerParams(
-            collective_id=0, has_side_effects=True, vmem_limit_bytes=60 * 2**20
+            collective_id=0, has_side_effects=True, vmem_limit_bytes=56 * 2**20
         ),
     )(tokens, dispatch_keys, expand_weight, reduce_weight, teacher)
     mixed, loss, grad = pl.pallas_call(
         hand_over,
         out_shape=out_shape,
-        in_specs=[any_spec, vmem_spec, vmem_spec],
-        out_specs=(any_spec, vmem_spec, vmem_spec),
-        scratch_shapes=[V((PART, D), bf16), dma((4,)), dma((4,))],
+        in_specs=[any_spec] * 3,
+        out_specs=(any_spec,) * 3,
+        scratch_shapes=[V(o.shape, o.dtype) for o in out_shape] + [dma((6,)), dma((6,))],
     )(mixed, loss, grad)
     return mixed, loss.reshape(()), grad
 

time: 83.7 us -> 82.1 us (0.981)
  Pallas kernels: 82.8 us -> 80.6 us
    pallas_call x1, Pallas kernels: 4.1 us -> 2.81 us  [body(): pl.pallas_call(hand_over, out_shape=out_shape, in_specs=[any_spec] * 3, o...]
    pallas_call x1, Pallas kernels: 78.7 us -> 77.8 us  [body(): pl.pallas_call(kernel, out_shape=out_shape, in_specs=[any_spec, vmem_spec...]
where the time goes in v3:
time: 82.1 us; the launch traced here: 81.3 us
  Pallas kernels  80.6 us (98%)
    pallas_call x1, Pallas kernels, body(): pl.pallas_call(kernel, out_shape=out_shape, in_specs=[any_spec, vmem_spec...  77.8 us
    pallas_call x1, Pallas kernels, body(): pl.pallas_call(hand_over, out_shape=out_shape, in_specs=[any_spec] * 3, o...  2.81 us

profile of v3, /device:TPU:1, one launch (start us, length us, event | category | flops | bytes accessed | tf_op | source)
XLA Modules:
  0.0 81.3 jit_solution(9819647728694041594)
XLA Ops:
  0.6 77.8 %shard_map.76 = (bf16[448,1536]{1,0:T(8,128)(2,1)}, f32[1,1]{1,0:T(1,128)}, f32[4,1536]{1,0:T(4,128)}) custom-call(bf16[3584,1536]{1,0:T(8,128)(2,1)} %tokens_h.1, bf16[4,1536]{1,0:T(4,128)(2,1)} %keys.1, bf16[4,1536,512]{2,1,0:T(8,128)(2,1)} %expand_h.1, bf16[4,512,1536]{2,1,0:T(8,128)(2,1)} %reduce_h.1, bf16[448,1536]{1,0:T(8,128)(2,1)} %teacher_h.1), custom_call_target="tpu_custom_call" | custom-call | tf_op jit(solution)/shard_map/pallas_call | solution.py:461
  78.4 2.8 %shard_map.77 = (bf16[448,1536]{1,0:T(8,128)(2,1)}, f32[1,1]{1,0:T(1,128)}, f32[4,1536]{1,0:T(4,128)}) custom-call(bf16[448,1536]{1,0:T(8,128)(2,1)} %get-tuple-element.9.refs_0_, f32[1,1]{1,0:T(1,128)} %get-tuple-element.10.refs_1_, f32[4,1536]{1,0:T(4,128)} %get-tuple-element.11.refs_2_), custom_call_target="tpu_custom_call" | custom-call | tf_op jit(solution)/shard_map/pallas_call | solution.py:491

commit v4 on v3

--- a/solution.py
+++ b/solution.py
@@ -14,7 +14,7 @@
 WIDE = 512
 LANES = 128
 Q = PARTS * LANES
-CHUNK = 1792
+CHUNK = 3584
 gelu_coef = 0.7978845608028654
 cube_coef = 0.044715
 
@@ -100,7 +100,7 @@
         pl.semaphore_signal(barrier, inc=1, device_id=(t2, z2 * 2 + c), device_id_type=MESH)
         return carry
 
-    lax.fori_loop(0, 63, greet, 0)
+    lax.fori_loop(0, 63, greet, 0, unroll=9)
     pl.semaphore_signal(barrier, inc=1, device_id=other, device_id_type=MESH)
 
     for n, (name, src, dst) in enumerate((
@@ -160,7 +160,7 @@
             remote(src_of(t2), recv_ref.at[t], send, recv, (t2, e))
             return carry
 
-        lax.fori_loop(0, TOK - 1, step, 0)
+        lax.fori_loop(0, TOK - 1, step, 0, unroll=True)
         flying.add(name + "_out", recv_ref.at[pl.ds(0, TOK - 1)], send)
         flying.add(name + "_in", recv_ref, recv)
 
@@ -173,7 +173,7 @@
             remote(src_of(z2 * TOK + t2), recv_ref.at[me], send, recv, (t2, z2 * 2 + c))
             return carry
 
-        lax.fori_loop(0, 63, step, 0)
+        lax.fori_loop(0, 63, step, 0, unroll=9)
         flying.add(name + "_out", recv_ref.at[pl.ds(0, 63)], send)
         flying.add(name + "_in", recv_ref, recv)
 
@@ -185,7 +185,7 @@
 
     def sum_of(ref, count):
         return lax.fori_loop(
-            0, count, lambda k, s: s + ref[k].astype(f32), jnp.zeros(ref.shape[1:], f32)
+            0, count, lambda k, s: s + ref[k].astype(f32), jnp.zeros(ref.shape[1:], f32), unroll=8
         )
 
     x16[...] = jnp.zeros((16, D), f32)

time: 82.1 us -> 80.2 us (0.977)
  Pallas kernels: 80.6 us -> 79.2 us
    pallas_call x1, Pallas kernels: 77.8 us -> 76.4 us  [body(): pl.pallas_call(kernel, out_shape=out_shape, in_specs=[any_spec, vmem_spec...]
where the time goes in v4:
time: 80.2 us; the launch traced here: 80 us
  Pallas kernels  79.2 us (99%)
    pallas_call x1, Pallas kernels, body(): pl.pallas_call(kernel, out_shape=out_shape, in_specs=[any_spec, vmem_spec...  76.4 us
    pallas_call x1, Pallas kernels, body(): pl.pallas_call(hand_over, out_shape=out_shape, in_specs=[any_spec] * 3, o...  2.81 us

profile of v4, /device:TPU:1, one launch (start us, length us, event | category | flops | bytes accessed | tf_op | source)
XLA Modules:
  0.0 80.0 jit_solution(2644538426057520723)
XLA Ops:
  0.6 76.4 %shard_map.76 = (bf16[448,1536]{1,0:T(8,128)(2,1)}, f32[1,1]{1,0:T(1,128)}, f32[4,1536]{1,0:T(4,128)}) custom-call(bf16[3584,1536]{1,0:T(8,128)(2,1)} %tokens_h.1, bf16[4,1536]{1,0:T(4,128)(2,1)} %keys.1, bf16[4,1536,512]{2,1,0:T(8,128)(2,1)} %expand_h.1, bf16[4,512,1536]{2,1,0:T(8,128)(2,1)} %reduce_h.1, bf16[448,1536]{1,0:T(8,128)(2,1)} %teacher_h.1), custom_call_target="tpu_custom_call" | custom-call | tf_op jit(solution)/shard_map/pallas_call | solution.py:461
  77.1 2.8 %shard_map.77 = (bf16[448,1536]{1,0:T(8,128)(2,1)}, f32[1,1]{1,0:T(1,128)}, f32[4,1536]{1,0:T(4,128)}) custom-call(bf16[448,1536]{1,0:T(8,128)(2,1)} %get-tuple-element.9.refs_0_, f32[1,1]{1,0:T(1,128)} %get-tuple-element.10.refs_1_, f32[4,1536]{1,0:T(4,128)} %get-tuple-element.11.refs_2_), custom_call_target="tpu_custom_call" | custom-call | tf_op jit(solution)/shard_map/pallas_call | solution.py:491

commit v5 on v4

--- a/solution.py
+++ b/solution.py
@@ -242,18 +242,6 @@
         msg_b[n] = spread(lines(part)).reshape(TOK, 16, LANES)
         to_tok(f"b{n}", lambda k: msg_b.at[n, k], recv_b.at[n], ssem_b.at[n], rsem_b.at[n])
 
-    for dz in range(1, 4):
-        flying.wait(f"keys_z{dz}")
-        key_cross(dz)
-    for dz in range(4):
-        flying.wait(f"keys_cross{dz}_in")
-    local = tokens.at[pl.ds(pl.multiple_of(e * PART, GROUP), PART)]
-    scores = nt(local[...], all_keys[...])
-    row_terms = jnp.exp(scores - jnp.max(scores, axis=1, keepdims=True))
-    comb_v = row_terms / jnp.sum(row_terms, axis=1, keepdims=True)
-    comb[...] = comb_v
-    comb_b[...] = comb_v.astype(bf16)
-
     flying.wait("b3_in")
     best = recv_b[PARTS, 0, :, 0:1].astype(f32)
     for k in range(1, TOK):
@@ -293,6 +281,18 @@
         out_msg[n] = packed_out[:, span(n)]
     for n in range(PARTS):
         to_all(f"o{n}", lambda k: out_msg.at[n], gath_o.at[n, 0], ssem_o.at[n], rsem_o.at[n])
+
+    for dz in range(1, 4):
+        flying.wait(f"keys_z{dz}")
+        key_cross(dz)
+    for dz in range(4):
+        flying.wait(f"keys_cross{dz}_in")
+    local = tokens.at[pl.ds(pl.multiple_of(e * PART, GROUP), PART)]
+    scores = nt(local[...], all_keys[...])
+    row_terms = jnp.exp(scores - jnp.max(scores, axis=1, keepdims=True))
+    comb_v = row_terms / jnp.sum(row_terms, axis=1, keepdims=True)
+    comb[...] = comb_v
+    comb_b[...] = comb_v.astype(bf16)
 
     flying.wait("teacher")
 

time: 80.2 us -> 78.9 us (0.984)
  Pallas kernels: 79.2 us -> 77.9 us
    pallas_call x1, Pallas kernels: 76.4 us -> 75.1 us  [body(): pl.pallas_call(kernel, out_shape=out_shape, in_specs=[any_spec, vmem_spec...]
where the time goes in v5:
time: 78.9 us; the launch traced here: 78.7 us
  Pallas kernels  77.9 us (99%)
  between operations  0.8 us (1%)
    pallas_call x1, Pallas kernels, body(): pl.pallas_call(kernel, out_shape=out_shape, in_specs=[any_spec, vmem_spec...  75.1 us
    pallas_call x1, Pallas kernels, body(): pl.pallas_call(hand_over, out_shape=out_shape, in_specs=[any_spec] * 3, o...  2.81 us

profile of v5, /device:TPU:1, one launch (start us, length us, event | category | flops | bytes accessed | tf_op | source)
XLA Modules:
  0.0 78.7 jit_solution(10282260065633046940)
XLA Ops:
  0.6 75.1 %shard_map.76 = (bf16[448,1536]{1,0:T(8,128)(2,1)}, f32[1,1]{1,0:T(1,128)}, f32[4,1536]{1,0:T(4,128)}) custom-call(bf16[3584,1536]{1,0:T(8,128)(2,1)} %tokens_h.1, bf16[4,1536]{1,0:T(4,128)(2,1)} %keys.1, bf16[4,1536,512]{2,1,0:T(8,128)(2,1)} %expand_h.1, bf16[4,512,1536]{2,1,0:T(8,128)(2,1)} %reduce_h.1, bf16[448,1536]{1,0:T(8,128)(2,1)} %teacher_h.1), custom_call_target="tpu_custom_call" | custom-call | tf_op jit(solution)/shard_map/pallas_call | solution.py:461
  75.8 2.8 %shard_map.77 = (bf16[448,1536]{1,0:T(8,128)(2,1)}, f32[1,1]{1,0:T(1,128)}, f32[4,1536]{1,0:T(4,128)}) custom-call(bf16[448,1536]{1,0:T(8,128)(2,1)} %get-tuple-element.9.refs_0_, f32[1,1]{1,0:T(1,128)} %get-tuple-element.10.refs_1_, f32[4,1536]{1,0:T(4,128)} %get-tuple-element.11.refs_2_), custom_call_target="tpu_custom_call" | custom-call | tf_op jit(solution)/shard_map/pallas_call | solution.py:491

commit v6 on v5

--- a/solution.py
+++ b/solution.py
@@ -417,10 +417,11 @@
         dprob = nt(all_keys[0:GROUP, :], tokens[pl.ds(at, CHUNK), :])
         weights[:, pl.ds(at, CHUNK)] = (terms[:, pl.ds(at, CHUNK)] * factor * dprob).astype(bf16)
 
-    flying.wait("e_in")
     for n in range(PARTS):
         cols = span(n, WIDE)
         part = nn(weights[...], tokens[:, cols])
+        if n == 0:
+            flying.wait("e_in")
         for k in range(4):
             part += recv_e[k, :, cols].astype(f32)
         msg_g[n] = spread(lines(part)).reshape(TOK, 16, LANES)

time: 78.9 us -> 79.2 us (level)
  no operation moved by 1% of the time
where the time goes in v6:
time: 79.2 us; the launch traced here: 79 us
  Pallas kernels  78.2 us (99%)
  between operations  0.8 us (1%)
    pallas_call x1, Pallas kernels, body(): pl.pallas_call(kernel, out_shape=out_shape, in_specs=[any_spec, vmem_spec...  75.4 us
    pallas_call x1, Pallas kernels, body(): pl.pallas_call(hand_over, out_shape=out_shape, in_specs=[any_spec] * 3, o...  2.81 us

profile of v6, /device:TPU:1, one launch (start us, length us, event | category | flops | bytes accessed | tf_op | source)
XLA Modules:
  0.0 79.0 jit_solution(18272676143516875795)
XLA Ops:
  0.6 75.4 %shard_map.76 = (bf16[448,1536]{1,0:T(8,128)(2,1)}, f32[1,1]{1,0:T(1,128)}, f32[4,1536]{1,0:T(4,128)}) custom-call(bf16[3584,1536]{1,0:T(8,128)(2,1)} %tokens_h.1, bf16[4,1536]{1,0:T(4,128)(2,1)} %keys.1, bf16[4,1536,512]{2,1,0:T(8,128)(2,1)} %expand_h.1, bf16[4,512,1536]{2,1,0:T(8,128)(2,1)} %reduce_h.1, bf16[448,1536]{1,0:T(8,128)(2,1)} %teacher_h.1), custom_call_target="tpu_custom_call" | custom-call | tf_op jit(solution)/shard_map/pallas_call | solution.py:462
  76.0 2.8 %shard_map.77 = (bf16[448,1536]{1,0:T(8,128)(2,1)}, f32[1,1]{1,0:T(1,128)}, f32[4,1536]{1,0:T(4,128)}) custom-call(bf16[448,1536]{1,0:T(8,128)(2,1)} %get-tuple-element.9.refs_0_, f32[1,1]{1,0:T(1,128)} %get-tuple-element.10.refs_1_, f32[4,1536]{1,0:T(4,128)} %get-tuple-element.11.refs_2_), custom_call_target="tpu_custom_call" | custom-call | tf_op jit(solution)/shard_map/pallas_call | solution.py:492
